TPU v7x, 512 devices: a whole 4x8x8 slice. The times are simulated.
512 devices in a mesh: ctx: 32 (over x, y), tp: 16 (over z, core).
Axes of the slice: x: 4, y: 8, z: 8, core: 2. Of those that a mesh axis runs over, the one named last changes fastest.
Arguments:
- prefix_x: bfloat16 [8192, 8192], P('ctx', 'tp'), may hold values from -6 to 6
- prefix_z: bfloat16 [8192, 8192], P('ctx', 'tp'), may hold values from -6 to 6
- prefix_bc: bfloat16 [8192, 256], P(('ctx', 'tp')), may hold values from -6 to 6
- prefix_dt: float32 [128, 8192], P('tp', 'ctx'), may hold values from -6 to 6
- branch_x: bfloat16 [8192, 8192], P('ctx', 'tp'), may hold values from -6 to 6
- branch_z: bfloat16 [8192, 8192], P('ctx', 'tp'), may hold values from -6 to 6
- branch_bc: bfloat16 [8192, 256], P(('ctx', 'tp')), may hold values from -6 to 6
- branch_dt: float32 [128, 8192], P('tp', 'ctx'), may hold values from -6 to 6
- conv_x: bfloat16 [4, 8192], P(None, 'tp'), may hold values from -3 to 3
- conv_bc: bfloat16 [4, 256], replicated, may hold values from -3 to 3
- decay_rate: float32 [128], P('tp'), may hold values from 2.4414063e-05 to 0.03
- skip: float32 [128], P('tp'), may hold values from 0.5 to 1.5
- norm_gain: float32 [8192], P('tp'), may hold values from 0.5 to 1.5
- bound_pos: int32 [8], replicated, may hold values from 0 to 8191
- branch_owner: int32 [64], replicated, may hold values from 0 to 31, as said below
- branch_parent: int32 [64], replicated, may hold values from 0 to 7
- branch_len: int32 [64], replicated, may hold values from 1 to 255, as said below
Outputs:
- prefix_out: bfloat16 [8192, 8192], P('ctx', 'tp')
- branch_out: bfloat16 [8192, 8192], P('ctx', 'tp')
Inputs may be any that keep to these rules, and one draw needn't show every extreme that they name: `branch_owner`: every block index 0 to 31 holds exactly 2 branches. `branch_len`: the branches of one block have lengths that sum to at most 256; in every draw some block's sum is exactly 256, and some branch has exactly 255 rows.
All inputs are finite; a program needn't handle non-finite values.
Results may differ from a plain program's by a relative error of at most 0.0034.
Values may be sent and summed in bfloat16 or wider, within the bound.
No kernel may reach another device: no remote copies, remote signals or barrier semaphores. Data moves between devices by JAX's collectives and lax.ppermute only.
A program may use at most 64 MiB of HBM per device.

v0:
```python
import jax
import jax.numpy as jnp
from jax import lax
from jax.sharding import PartitionSpec as P

NORM_GROUP = 8192
BR_PER = 2
EPSILON = 1e-05


def passed_along(value, axis, steps):
    count = lax.axis_size(axis)
    first, last = (max(0, -steps), min(count, count - steps))
    return lax.ppermute(value, axis, [(source, source + steps) for source in range(first, last)])


def conv_silu(lagged, weights):
    summed = weights[0].astype(jnp.float32)[None, :] * lagged[0].astype(jnp.float32)
    for tap_index in range(1, len(lagged)):
        summed = summed + weights[tap_index].astype(jnp.float32)[None, :] * lagged[
            tap_index
        ].astype(jnp.float32)
    return jax.nn.silu(summed).astype(jnp.bfloat16)


def split_conv(convolved, channels, head_count):
    length = convolved.shape[0]
    state_size = (convolved.shape[1] - channels) // 2
    values = convolved[:, :channels].reshape(length, head_count, channels // head_count)
    return (
        values,
        convolved[:, channels : channels + state_size],
        convolved[:, channels + state_size :],
    )


def decays(raw_steps, rates):
    step_size = jax.nn.softplus(raw_steps)
    log_decay = -rates[:, None] * step_size
    return (step_size, log_decay, jnp.cumsum(log_decay, axis=1))


def intra_block(values, b_rows, c_rows, step_size, cumulative, causal_mask):
    scores = jnp.dot(c_rows, b_rows.T, preferred_element_type=jnp.float32)
    exponent = jnp.where(causal_mask[None], cumulative[:, :, None] - cumulative[:, None, :], 0.0)
    mixing = jnp.where(
        causal_mask[None], scores[None] * jnp.exp(exponent) * step_size[:, None, :], 0.0
    ).astype(jnp.bfloat16)
    return jnp.einsum("hts,shp->thp", mixing, values, preferred_element_type=jnp.float32)


def local_states(values, b_rows, step_size, cumulative, positions):
    length = cumulative.shape[1]
    clipped = jnp.clip(positions, 0, length - 1)
    decay_end = jnp.take(cumulative, clipped, axis=1)
    row_index = jnp.arange(length, dtype=jnp.int32)
    inside = row_index[None, :] <= positions[:, None]
    exponent = jnp.where(inside[:, None, :], decay_end.T[:, :, None] - cumulative[None], 0.0)
    weight = jnp.where(inside[:, None, :], jnp.exp(exponent) * step_size[None], 0.0)
    weighted = (
        jnp.transpose(weight, (0, 2, 1))[:, :, :, None] * values[None].astype(jnp.float32)
    ).astype(jnp.bfloat16)
    return jnp.einsum("jshp,sn->jhpn", weighted, b_rows, preferred_element_type=jnp.float32)


def from_state(c_rows, state, weight):
    result = jnp.einsum(
        "tn,hpn->thp", c_rows.astype(jnp.float32), state, precision=lax.Precision.HIGHEST
    )
    return result * weight.T[:, :, None]


def finish(mixed_out, values, skip, gate_rows, gain):
    length = mixed_out.shape[0]
    mixed_out = mixed_out + skip[None, :, None] * values.astype(jnp.float32)
    gated = mixed_out.reshape(length, -1) * jax.nn.silu(gate_rows.astype(jnp.float32))
    partial_squares = jnp.sum(gated * gated, axis=1, keepdims=True)
    total_squares = lax.psum(partial_squares, "tp")
    factor = lax.rsqrt(total_squares / NORM_GROUP + EPSILON)
    return (gated * factor * gain[None, :]).astype(jnp.bfloat16)


def layout(owner_index, branch_owner, branch_parent, branch_len, length):
    owned = (branch_owner == owner_index).astype(jnp.int32)
    owned_rank = jnp.cumsum(owned) - 1
    owned_lengths = owned * branch_len
    starts = jnp.cumsum(owned_lengths) - owned_lengths
    branch_slot = jnp.arange(BR_PER, dtype=jnp.int32)
    chosen = owned[None, :] * (owned_rank[None, :] == branch_slot[:, None]).astype(jnp.int32)
    segment_length = jnp.sum(chosen * branch_len[None, :], axis=1)
    segment_start = jnp.sum(chosen * starts[None, :], axis=1)
    parents = jnp.sum(chosen * branch_parent[None, :], axis=1)
    row_index = jnp.arange(length, dtype=jnp.int32)
    inside = (
        (row_index[None, :] >= segment_start[:, None])
        & (row_index[None, :] < (segment_start + segment_length)[:, None])
    ).astype(jnp.int32)
    live_count = jnp.sum(inside, axis=0)
    segment = jnp.sum(inside * branch_slot[:, None], axis=0) + BR_PER * (1 - live_count)
    offset = row_index - jnp.sum(inside * segment_start[:, None], axis=0)
    return (segment, offset, live_count > 0, parents)


def branch_block(
    joined_rows,
    gate_rows,
    raw_steps,
    all_states,
    all_tails,
    weights,
    rates,
    skip,
    gain,
    owner_index,
    branch_owner,
    branch_parent,
    branch_len,
):
    length, row_width = joined_rows.shape
    channels = gate_rows.shape[1]
    head_count = rates.shape[0]
    tail_count = weights.shape[0] - 1
    segment, offset, live_rows, parents = layout(
        owner_index, branch_owner, branch_parent, branch_len, length
    )
    seed_states = jnp.take(all_states, parents, axis=0)
    tail_rows = jnp.take(all_tails, parents, axis=0).reshape(-1, row_width).astype(jnp.bfloat16)
    column = jnp.arange(tail_rows.shape[0], dtype=jnp.int32)
    column_segment = column // tail_count
    column_row = column % tail_count
    lagged = []
    for tap_index in range(tail_count + 1):
        shift_rows = tail_count - tap_index
        if shift_rows == 0:
            lagged.append(joined_rows)
        else:
            shifted = jnp.concatenate(
                [
                    jnp.zeros((shift_rows, row_width), jnp.bfloat16),
                    joined_rows[: length - shift_rows],
                ],
                axis=0,
            )
            local_rows = jnp.where(
                (offset >= shift_rows)[:, None], shifted, jnp.zeros_like(shifted)
            )
            picker = (
                (segment[:, None] == column_segment[None, :])
                & (offset[:, None] < shift_rows)
                & (column_row[None, :] == tail_count - shift_rows + offset[:, None])
            ).astype(jnp.bfloat16)
            tail_part = jnp.dot(picker, tail_rows, preferred_element_type=jnp.float32).astype(
                jnp.bfloat16
            )
            lagged.append(local_rows + tail_part)
    values, b_rows, c_rows = split_conv(conv_silu(lagged, weights), channels, head_count)
    step_size, log_decay, cumulative = decays(raw_steps, rates)
    row_index = jnp.arange(length, dtype=jnp.int32)
    causal_mask = (
        (segment[:, None] == segment[None, :])
        & live_rows[:, None]
        & (row_index[None, :] <= row_index[:, None])
    )
    mixed_out = intra_block(values, b_rows, c_rows, step_size, cumulative, causal_mask)
    first_rows = jnp.clip(row_index - offset, 0, length - 1)
    start_log = jnp.take(cumulative - log_decay, first_rows, axis=1)
    seed_weight = jnp.where(
        live_rows[None, :], jnp.exp(jnp.where(live_rows[None, :], cumulative - start_log, 0.0)), 0.0
    )
    for branch_slot in range(seed_states.shape[0]):
        portion = from_state(c_rows, seed_states[branch_slot], seed_weight)
        mixed_out = mixed_out + jnp.where((segment == branch_slot)[:, None, None], portion, 0.0)
    result = finish(mixed_out, values, skip, gate_rows, gain)
    return jnp.where(live_rows[:, None], result, jnp.zeros_like(result))


def body(
    prefix_x,
    prefix_z,
    prefix_bc,
    prefix_dt,
    branch_x,
    branch_z,
    branch_bc,
    branch_dt,
    conv_x,
    conv_bc,
    decay_rate,
    skip,
    norm_gain,
    bound_pos,
    branch_owner,
    branch_parent,
    branch_len,
):
    prefix_gathered, branch_gathered = (
        lax.all_gather(prefix_bc, "tp", axis=0, tiled=True),
        lax.all_gather(branch_bc, "tp", axis=0, tiled=True),
    )
    length = prefix_x.shape[0]
    channels = prefix_x.shape[1]
    head_count = decay_rate.shape[0]
    weights = jnp.concatenate([conv_x, conv_bc], axis=1)
    tail_count = weights.shape[0] - 1
    joined_rows = jnp.concatenate([prefix_x, prefix_gathered], axis=1)
    before = passed_along(joined_rows[length - tail_count :], "ctx", 1)
    extended = jnp.concatenate([before, joined_rows], axis=0)
    lagged = [extended[tap_index : tap_index + length] for tap_index in range(tail_count + 1)]
    values, b_rows, c_rows = split_conv(conv_silu(lagged, weights), channels, head_count)
    step_size, log_decay, cumulative = decays(prefix_dt, decay_rate)
    row_index = jnp.arange(length, dtype=jnp.int32)
    causal_mask = row_index[None, :] <= row_index[:, None]
    mixed_out = intra_block(values, b_rows, c_rows, step_size, cumulative, causal_mask)
    owner_index = lax.axis_index("ctx")
    local_at = jnp.where(bound_pos // length == owner_index, bound_pos - owner_index * length, -1)
    positions = jnp.concatenate([local_at, jnp.full((1,), length - 1, jnp.int32)])
    states = local_states(values, b_rows, step_size, cumulative, positions)
    bound_count = bound_pos.shape[0]
    end_state = states[bound_count]
    end_decay = jnp.exp(cumulative[:, -1])

    def carry_step(unused, state):
        return passed_along(end_decay[:, None, None] * state + end_state, "ctx", 1)

    entering = lax.fori_loop(0, lax.axis_size("ctx") - 1, carry_step, jnp.zeros_like(end_state))
    mixed_out = mixed_out + from_state(c_rows, entering, jnp.exp(cumulative))
    prefix_out = finish(mixed_out, values, skip, prefix_z, norm_gain)
    held_here = local_at >= 0
    decay_at = jnp.exp(jnp.take(cumulative, jnp.clip(local_at, 0, length - 1), axis=1))
    candidate = jnp.where(
        held_here[:, None, None, None],
        decay_at.T[:, :, None, None] * entering[None] + states[:bound_count],
        0.0,
    )
    tail_index = (local_at[:, None] + 1 + jnp.arange(tail_count, dtype=jnp.int32)[None, :]).reshape(
        -1
    )
    held_rows = jnp.repeat(held_here, tail_count)
    picker = (
        (jnp.arange(length + tail_count, dtype=jnp.int32)[None, :] == tail_index[:, None])
        & held_rows[:, None]
    ).astype(jnp.bfloat16)
    tail_rows = jnp.dot(picker, extended, preferred_element_type=jnp.float32).reshape(
        bound_count, tail_count, -1
    )
    all_states, all_tails = lax.psum((candidate, tail_rows), "ctx")
    branch_joined = jnp.concatenate([branch_x, branch_gathered], axis=1)
    branch_out = branch_block(
        branch_joined,
        branch_z,
        branch_dt,
        all_states,
        all_tails,
        weights,
        decay_rate,
        skip,
        norm_gain,
        owner_index,
        branch_owner,
        branch_parent,
        branch_len,
    )
    return (prefix_out, branch_out)


def solution(mesh):
    in_specs = (
        P("ctx", "tp"),
        P("ctx", "tp"),
        P(("ctx", "tp"), None),
        P("tp", "ctx"),
        P("ctx", "tp"),
        P("ctx", "tp"),
        P(("ctx", "tp"), None),
        P("tp", "ctx"),
        P(None, "tp"),
        P(),
        P("tp"),
        P("tp"),
        P("tp"),
        P(),
        P(),
        P(),
        P(),
    )
    out_specs = (P("ctx", "tp"), P("ctx", "tp"))
    return jax.shard_map(body, mesh=mesh, in_specs=in_specs, out_specs=out_specs, check_vma=False)
```

profile of v0, /device:TPU:1, one launch (start us, length us, event | category | flops | bytes accessed | tf_op | source)
XLA Modules:
  0.0 639.3 jit_solution(6690966973142288056)
XLA Ops:
  8.3 25.1 %all_gather.6 = bf16[256,256]{1,0:T(8,128)(2,1)S(1)} all-gather(bf16[16,256]{1,0:T(8,128)(2,1)} %param.21), channel_id=1, replica_groups=mesh['ctx'=32,'tp'=16] {'tp'}, dimensions={0}, use_global_device_ids=true | all-gather | bytes 139264 | tf_op jit(solution)/shard_map/all_gather | solution.py:197
  50.8 14.8 %all_gather.7 = bf16[256,256]{1,0:T(8,128)(2,1)S(1)} all-gather(bf16[16,256]{1,0:T(8,128)(2,1)S(1)} %copy-done.27), channel_id=1, replica_groups=mesh['ctx'=32,'tp'=16] {'tp'}, dimensions={0}, use_global_device_ids=true | all-gather | bytes 139264 | tf_op jit(solution)/shard_map/all_gather | solution.py:198
  74.3 305.5 %while.10 = (s32[]{:T(128)}, f32[8,64,128]{2,1,0:T(8,128)S(1)}, f32[8]{0:T(128)}, f32[8,64,128]{2,1,0:T(8,128)S(1)}, s32[]{:T(128)}) while((s32[]{:T(128)}, f32[8,64,128]{2,1,0:T(8,128)S(1)}, f32[8]{0:T(128)}, f32[8,64,128]{2,1,0:T(8,128)S(1)}, s32[]{:T(128)}) %tuple.49), condition=%wide.region_3.4_spmd, body=%wide.region_2.3_spmd.sunk | while | flops 131074 | bytes 1835141 | solution.py:225
  78.2 5.5 collective-permute-done
  126.8 5.3 collective-permute-start
  154.9 5.5 collective-permute-start
  166.1 5.9 collective-permute-start
  172.0 6.0 collective-permute-done
  178.7 5.4 collective-permute-start
  207.2 5.3 collective-permute-start
  225.8 5.5 collective-permute-start
  254.5 5.3 collective-permute-start
  269.9 5.6 collective-permute-done
  280.4 5.7 collective-permute-done
  291.9 5.8 collective-permute-done
  298.4 6.9 %collective-permute-start = (f32[8,64,128]{2,1,0:T(8,128)S(1)}, f32[8,64,128]{2,1,0:T(8,128)S(1)}, u32[]{:S(2)}, u32[]{:S(2)}) collective-permute-start(f32[8,64,128]{2,1,0:T(8,128)S(1)} %multiply_add_fusion.4), channel_id=1, source_target_pairs={{0,16},{16,32},{32,48},{48,64},{64,80},{80,96},{96,112},{112,128},... | collective-permute-start | bytes 786440 | tf_op jit(solution)/shard_map/while/body/eval_jaxpr/ppermute | solution.py:14
  311.0 6.1 collective-permute-start
  321.5 6.8 %collective-permute-start = (f32[8,64,128]{2,1,0:T(8,128)S(1)}, f32[8,64,128]{2,1,0:T(8,128)S(1)}, u32[]{:S(2)}, u32[]{:S(2)}) collective-permute-start(f32[8,64,128]{2,1,0:T(8,128)S(1)} %multiply_add_fusion.4), channel_id=1, source_target_pairs={{0,16},{16,32},{32,48},{48,64},{64,80},{80,96},{96,112},{112,128},... | collective-permute-start | bytes 786440 | tf_op jit(solution)/shard_map/while/body/eval_jaxpr/ppermute | solution.py:14
  341.3 5.3 collective-permute-start
  359.6 6.1 collective-permute-start
  369.7 6.2 collective-permute-start
  385.2 129.7 %psum.29 = bf16[8,3,768]{2,1,0:T(4,128)(2,1)S(1)} all-reduce(f32[8,3,768]{2,1,0:T(4,128)S(1)} %reshape.508), channel_id=1, replica_groups=mesh['ctx'=32,'tp'=16] {'ctx'}, use_global_device_ids=true, to_apply=%region_14.15 | all-reduce | flops 18432 | bytes 110592 | tf_op jit(solution)/shard_map/psum | solution.py:246
  520.7 75.1 %all-reduce.6.cloned.1.call-done = f32[8,8,64,128]{3,2,1,0:T(8,128)} async-done(((f32[8,8,64,128]{3,2,1,0:T(8,128)}), f32[8,8,64,128]{3,2,1,0:T(8,128)}) %all-reduce.6.cloned.1.call-update) | async-done | bytes 2097168 | tf_op jit(solution)/shard_map/psum | solution.py:246
  602.0 28.6 %all-reduce.3 = (f32[256,1]{0,1:T(1,128)S(1)}, f32[256,1]{0,1:T(1,128)S(1)}) all-reduce(f32[256,1]{0,1:T(1,128)S(1)} %bitcast.99, f32[256,1]{0,1:T(1,128)S(1)} %bitcast.102), channel_id=1, replica_groups=mesh['ctx'=32,'tp'=16] {'tp'}, use_global_device_ids=true, to_apply=%region_5.6 | all-reduce | flops 512 | bytes 4096 | tf_op jit(solution)/shard_map/psum | solution.py:78
  (311 shorter events, 246.1 us)
Async XLA Ops:
  7.2 588.5 %all-reduce.6.cloned.1.call-start = ((), (), s32[]{:S(2)}) async-start(), calls=%async_computation | async-start | bytes 4194304 | tf_op jit(solution)/shard_map/psum | solution.py:246
  33.5 38.7 %collective-permute-start.1 = (bf16[3,768]{1,0:T(4,128)(2,1)S(1)}, bf16[3,768]{1,0:T(4,128)(2,1)S(1)}, u32[]{:S(2)}, u32[]{:S(2)}) collective-permute-start(bf16[3,768]{1,0:T(4,128)(2,1)S(1)} %slice.119), channel_id=1, source_target_pairs={{0,16},{16,32},{32,48},{48,64},{64,80},{80,96},{96,112},{112,128},... | collective-permute-start | bytes 13832 | tf_op jit(solution)/shard_map/ppermute | solution.py:14
  75.0 8.8 %collective-permute-start = (f32[8,64,128]{2,1,0:T(8,128)S(1)}, f32[8,64,128]{2,1,0:T(8,128)S(1)}, u32[]{:S(2)}, u32[]{:S(2)}) collective-permute-start(f32[8,64,128]{2,1,0:T(8,128)S(1)} %multiply_add_fusion.4), channel_id=1, source_target_pairs={{0,16},{16,32},{32,48},{48,64},{64,80},{80,96},{96,112},{112,128},... | collective-permute-start | bytes 786440 | tf_op jit(solution)/shard_map/while/body/eval_jaxpr/ppermute | solution.py:14
  84.4 8.7 %collective-permute-start = (f32[8,64,128]{2,1,0:T(8,128)S(1)}, f32[8,64,128]{2,1,0:T(8,128)S(1)}, u32[]{:S(2)}, u32[]{:S(2)}) collective-permute-start(f32[8,64,128]{2,1,0:T(8,128)S(1)} %multiply_add_fusion.4), channel_id=1, source_target_pairs={{0,16},{16,32},{32,48},{48,64},{64,80},{80,96},{96,112},{112,128},... | collective-permute-start | bytes 786440 | tf_op jit(solution)/shard_map/while/body/eval_jaxpr/ppermute | solution.py:14
  126.8 8.6 %collective-permute-start = (f32[8,64,128]{2,1,0:T(8,128)S(1)}, f32[8,64,128]{2,1,0:T(8,128)S(1)}, u32[]{:S(2)}, u32[]{:S(2)}) collective-permute-start(f32[8,64,128]{2,1,0:T(8,128)S(1)} %multiply_add_fusion.4), channel_id=1, source_target_pairs={{0,16},{16,32},{32,48},{48,64},{64,80},{80,96},{96,112},{112,128},... | collective-permute-start | bytes 786440 | tf_op jit(solution)/shard_map/while/body/eval_jaxpr/ppermute | solution.py:14
  145.1 9.1 %collective-permute-start = (f32[8,64,128]{2,1,0:T(8,128)S(1)}, f32[8,64,128]{2,1,0:T(8,128)S(1)}, u32[]{:S(2)}, u32[]{:S(2)}) collective-permute-start(f32[8,64,128]{2,1,0:T(8,128)S(1)} %multiply_add_fusion.4), channel_id=1, source_target_pairs={{0,16},{16,32},{32,48},{48,64},{64,80},{80,96},{96,112},{112,128},... | collective-permute-start | bytes 786440 | tf_op jit(solution)/shard_map/while/body/eval_jaxpr/ppermute | solution.py:14
  154.9 10.5 %collective-permute-start = (f32[8,64,128]{2,1,0:T(8,128)S(1)}, f32[8,64,128]{2,1,0:T(8,128)S(1)}, u32[]{:S(2)}, u32[]{:S(2)}) collective-permute-start(f32[8,64,128]{2,1,0:T(8,128)S(1)} %multiply_add_fusion.4), channel_id=1, source_target_pairs={{0,16},{16,32},{32,48},{48,64},{64,80},{80,96},{96,112},{112,128},... | collective-permute-start | bytes 786440 | tf_op jit(solution)/shard_map/while/body/eval_jaxpr/ppermute | solution.py:14
  166.1 11.9 %collective-permute-start = (f32[8,64,128]{2,1,0:T(8,128)S(1)}, f32[8,64,128]{2,1,0:T(8,128)S(1)}, u32[]{:S(2)}, u32[]{:S(2)}) collective-permute-start(f32[8,64,128]{2,1,0:T(8,128)S(1)} %multiply_add_fusion.4), channel_id=1, source_target_pairs={{0,16},{16,32},{32,48},{48,64},{64,80},{80,96},{96,112},{112,128},... | collective-permute-start | bytes 786440 | tf_op jit(solution)/shard_map/while/body/eval_jaxpr/ppermute | solution.py:14
  178.7 10.1 %collective-permute-start = (f32[8,64,128]{2,1,0:T(8,128)S(1)}, f32[8,64,128]{2,1,0:T(8,128)S(1)}, u32[]{:S(2)}, u32[]{:S(2)}) collective-permute-start(f32[8,64,128]{2,1,0:T(8,128)S(1)} %multiply_add_fusion.4), channel_id=1, source_target_pairs={{0,16},{16,32},{32,48},{48,64},{64,80},{80,96},{96,112},{112,128},... | collective-permute-start | bytes 786440 | tf_op jit(solution)/shard_map/while/body/eval_jaxpr/ppermute | solution.py:14
  189.5 8.8 %collective-permute-start = (f32[8,64,128]{2,1,0:T(8,128)S(1)}, f32[8,64,128]{2,1,0:T(8,128)S(1)}, u32[]{:S(2)}, u32[]{:S(2)}) collective-permute-start(f32[8,64,128]{2,1,0:T(8,128)S(1)} %multiply_add_fusion.4), channel_id=1, source_target_pairs={{0,16},{16,32},{32,48},{48,64},{64,80},{80,96},{96,112},{112,128},... | collective-permute-start | bytes 786440 | tf_op jit(solution)/shard_map/while/body/eval_jaxpr/ppermute | solution.py:14
  207.2 8.6 %collective-permute-start = (f32[8,64,128]{2,1,0:T(8,128)S(1)}, f32[8,64,128]{2,1,0:T(8,128)S(1)}, u32[]{:S(2)}, u32[]{:S(2)}) collective-permute-start(f32[8,64,128]{2,1,0:T(8,128)S(1)} %multiply_add_fusion.4), channel_id=1, source_target_pairs={{0,16},{16,32},{32,48},{48,64},{64,80},{80,96},{96,112},{112,128},... | collective-permute-start | bytes 786440 | tf_op jit(solution)/shard_map/while/body/eval_jaxpr/ppermute | solution.py:14
  216.5 8.6 %collective-permute-start = (f32[8,64,128]{2,1,0:T(8,128)S(1)}, f32[8,64,128]{2,1,0:T(8,128)S(1)}, u32[]{:S(2)}, u32[]{:S(2)}) collective-permute-start(f32[8,64,128]{2,1,0:T(8,128)S(1)} %multiply_add_fusion.4), channel_id=1, source_target_pairs={{0,16},{16,32},{32,48},{48,64},{64,80},{80,96},{96,112},{112,128},... | collective-permute-start | bytes 786440 | tf_op jit(solution)/shard_map/while/body/eval_jaxpr/ppermute | solution.py:14
  225.8 8.8 %collective-permute-start = (f32[8,64,128]{2,1,0:T(8,128)S(1)}, f32[8,64,128]{2,1,0:T(8,128)S(1)}, u32[]{:S(2)}, u32[]{:S(2)}) collective-permute-start(f32[8,64,128]{2,1,0:T(8,128)S(1)} %multiply_add_fusion.4), channel_id=1, source_target_pairs={{0,16},{16,32},{32,48},{48,64},{64,80},{80,96},{96,112},{112,128},... | collective-permute-start | bytes 786440 | tf_op jit(solution)/shard_map/while/body/eval_jaxpr/ppermute | solution.py:14
  244.3 9.4 %collective-permute-start = (f32[8,64,128]{2,1,0:T(8,128)S(1)}, f32[8,64,128]{2,1,0:T(8,128)S(1)}, u32[]{:S(2)}, u32[]{:S(2)}) collective-permute-start(f32[8,64,128]{2,1,0:T(8,128)S(1)} %multiply_add_fusion.4), channel_id=1, source_target_pairs={{0,16},{16,32},{32,48},{48,64},{64,80},{80,96},{96,112},{112,128},... | collective-permute-start | bytes 786440 | tf_op jit(solution)/shard_map/while/body/eval_jaxpr/ppermute | solution.py:14
  254.5 10.4 %collective-permute-start = (f32[8,64,128]{2,1,0:T(8,128)S(1)}, f32[8,64,128]{2,1,0:T(8,128)S(1)}, u32[]{:S(2)}, u32[]{:S(2)}) collective-permute-start(f32[8,64,128]{2,1,0:T(8,128)S(1)} %multiply_add_fusion.4), channel_id=1, source_target_pairs={{0,16},{16,32},{32,48},{48,64},{64,80},{80,96},{96,112},{112,128},... | collective-permute-start | bytes 786440 | tf_op jit(solution)/shard_map/while/body/eval_jaxpr/ppermute | solution.py:14
  265.5 10.0 %collective-permute-start = (f32[8,64,128]{2,1,0:T(8,128)S(1)}, f32[8,64,128]{2,1,0:T(8,128)S(1)}, u32[]{:S(2)}, u32[]{:S(2)}) collective-permute-start(f32[8,64,128]{2,1,0:T(8,128)S(1)} %multiply_add_fusion.4), channel_id=1, source_target_pairs={{0,16},{16,32},{32,48},{48,64},{64,80},{80,96},{96,112},{112,128},... | collective-permute-start | bytes 786440 | tf_op jit(solution)/shard_map/while/body/eval_jaxpr/ppermute | solution.py:14
  276.2 9.8 %collective-permute-start = (f32[8,64,128]{2,1,0:T(8,128)S(1)}, f32[8,64,128]{2,1,0:T(8,128)S(1)}, u32[]{:S(2)}, u32[]{:S(2)}) collective-permute-start(f32[8,64,128]{2,1,0:T(8,128)S(1)} %multiply_add_fusion.4), channel_id=1, source_target_pairs={{0,16},{16,32},{32,48},{48,64},{64,80},{80,96},{96,112},{112,128},... | collective-permute-start | bytes 786440 | tf_op jit(solution)/shard_map/while/body/eval_jaxpr/ppermute | solution.py:14
  286.7 11.0 %collective-permute-start = (f32[8,64,128]{2,1,0:T(8,128)S(1)}, f32[8,64,128]{2,1,0:T(8,128)S(1)}, u32[]{:S(2)}, u32[]{:S(2)}) collective-permute-start(f32[8,64,128]{2,1,0:T(8,128)S(1)} %multiply_add_fusion.4), channel_id=1, source_target_pairs={{0,16},{16,32},{32,48},{48,64},{64,80},{80,96},{96,112},{112,128},... | collective-permute-start | bytes 786440 | tf_op jit(solution)/shard_map/while/body/eval_jaxpr/ppermute | solution.py:14
  298.4 11.9 %collective-permute-start = (f32[8,64,128]{2,1,0:T(8,128)S(1)}, f32[8,64,128]{2,1,0:T(8,128)S(1)}, u32[]{:S(2)}, u32[]{:S(2)}) collective-permute-start(f32[8,64,128]{2,1,0:T(8,128)S(1)} %multiply_add_fusion.4), channel_id=1, source_target_pairs={{0,16},{16,32},{32,48},{48,64},{64,80},{80,96},{96,112},{112,128},... | collective-permute-start | bytes 786440 | tf_op jit(solution)/shard_map/while/body/eval_jaxpr/ppermute | solution.py:14
  311.0 9.8 %collective-permute-start = (f32[8,64,128]{2,1,0:T(8,128)S(1)}, f32[8,64,128]{2,1,0:T(8,128)S(1)}, u32[]{:S(2)}, u32[]{:S(2)}) collective-permute-start(f32[8,64,128]{2,1,0:T(8,128)S(1)} %multiply_add_fusion.4), channel_id=1, source_target_pairs={{0,16},{16,32},{32,48},{48,64},{64,80},{80,96},{96,112},{112,128},... | collective-permute-start | bytes 786440 | tf_op jit(solution)/shard_map/while/body/eval_jaxpr/ppermute | solution.py:14
  321.5 10.1 %collective-permute-start = (f32[8,64,128]{2,1,0:T(8,128)S(1)}, f32[8,64,128]{2,1,0:T(8,128)S(1)}, u32[]{:S(2)}, u32[]{:S(2)}) collective-permute-start(f32[8,64,128]{2,1,0:T(8,128)S(1)} %multiply_add_fusion.4), channel_id=1, source_target_pairs={{0,16},{16,32},{32,48},{48,64},{64,80},{80,96},{96,112},{112,128},... | collective-permute-start | bytes 786440 | tf_op jit(solution)/shard_map/while/body/eval_jaxpr/ppermute | solution.py:14
  341.3 8.6 %collective-permute-start = (f32[8,64,128]{2,1,0:T(8,128)S(1)}, f32[8,64,128]{2,1,0:T(8,128)S(1)}, u32[]{:S(2)}, u32[]{:S(2)}) collective-permute-start(f32[8,64,128]{2,1,0:T(8,128)S(1)} %multiply_add_fusion.4), channel_id=1, source_target_pairs={{0,16},{16,32},{32,48},{48,64},{64,80},{80,96},{96,112},{112,128},... | collective-permute-start | bytes 786440 | tf_op jit(solution)/shard_map/while/body/eval_jaxpr/ppermute | solution.py:14
  359.6 9.4 %collective-permute-start = (f32[8,64,128]{2,1,0:T(8,128)S(1)}, f32[8,64,128]{2,1,0:T(8,128)S(1)}, u32[]{:S(2)}, u32[]{:S(2)}) collective-permute-start(f32[8,64,128]{2,1,0:T(8,128)S(1)} %multiply_add_fusion.4), channel_id=1, source_target_pairs={{0,16},{16,32},{32,48},{48,64},{64,80},{80,96},{96,112},{112,128},... | collective-permute-start | bytes 786440 | tf_op jit(solution)/shard_map/while/body/eval_jaxpr/ppermute | solution.py:14
  369.7 10.0 %collective-permute-start = (f32[8,64,128]{2,1,0:T(8,128)S(1)}, f32[8,64,128]{2,1,0:T(8,128)S(1)}, u32[]{:S(2)}, u32[]{:S(2)}) collective-permute-start(f32[8,64,128]{2,1,0:T(8,128)S(1)} %multiply_add_fusion.4), channel_id=1, source_target_pairs={{0,16},{16,32},{32,48},{48,64},{64,80},{80,96},{96,112},{112,128},... | collective-permute-start | bytes 786440 | tf_op jit(solution)/shard_map/while/body/eval_jaxpr/ppermute | solution.py:14
  (67 other events, 3427.8 us)
Sparse Core Ops, SparseCore 0:
  382.3 213.4 all-reduce.5
where the time goes:
time: 641 us; the launch traced here: 639 us
  waiting for transfers between devices  200 us (31%)
  blocking collectives  198 us (31%)
  starting transfers between devices  161 us (25%)
  other arithmetic  38.4 us (6%)
  local copies, waits for them, and re-layouts  16.2 us (3%)
  between operations  15.2 us (2%)
  matrix products  9.01 us (1%)
    ppermute x32, starting transfers between devices, passed_along(): lax.ppermute(value, axis, [(source, source + steps) for source in range(f...  161 us
    psum x1, blocking collectives, body(): all_states, all_tails = lax.psum((candidate, tail_rows), 'ctx')  130 us
    ppermute x32, waiting for transfers between devices, passed_along(): lax.ppermute(value, axis, [(source, source + steps) for source in range(f...  125 us
    psum x1, waiting for transfers between devices, body(): all_states, all_tails = lax.psum((candidate, tail_rows), 'ctx')  75.1 us
    psum x1, blocking collectives, finish(): total_squares = lax.psum(partial_squares, 'tp')  28.6 us
    all_gather x1, blocking collectives, body(): lax.all_gather(prefix_bc, 'tp', axis=0, tiled=True)  25.1 us
    add x31, other arithmetic, carry_step(): return passed_along(end_decay[:, None, None] * state + end_state, 'ctx', 1)  21.6 us
    all_gather x1, blocking collectives, body(): lax.all_gather(branch_bc, 'tp', axis=0, tiled=True)  14.8 us
  transfers between devices with their start and end apart: 33, of which 32 were waited for; matrix products, arithmetic and copies ran while one was open for 4% of the time, Pallas kernels for 0%

commit v1 on v0

--- a/solution.py
+++ b/solution.py
@@ -193,8 +193,20 @@
     branch_parent,
     branch_len,
 ):
+
+    def _name_plane(frame_in):
+        return jnp.concatenate(
+            jax.lax.all_to_all(
+                jnp.stack(jax.lax.axis_size("tp") * [frame_in], axis=0),
+                "tp",
+                split_axis=0,
+                concat_axis=0,
+            ),
+            0,
+        )
+
     prefix_gathered, branch_gathered = (
-        lax.all_gather(prefix_bc, "tp", axis=0, tiled=True),
+        _name_plane(prefix_bc),
         lax.all_gather(branch_bc, "tp", axis=0, tiled=True),
     )
     length = prefix_x.shape[0]

time: 641 us -> 637 us (level)
  blocking collectives: 198 us -> 176 us
  starting transfers between devices: 161 us -> 173 us
    all_gather x1 -> x0, blocking collectives: 25.1 us -> none  [body(): lax.all_gather(prefix_bc, 'tp', axis=0, tiled=True)]
    all_to_all x0 -> x1, starting transfers between devices: none -> 11.8 us  [_name_plane(): jax.lax.all_to_all(jnp.stack(jax.lax.axis_size('tp') * [frame_in], axis=0...]
  transfers between devices with their start and end apart: 33 -> 34, of which waited for: 32 -> 32; matrix products, arithmetic and copies ran while one was open for 4% -> 5% of each run, Pallas kernels for 0% -> 0%
where the time goes in v1:
time: 637 us; the launch traced here: 635 us
  waiting for transfers between devices  202 us (32%)
  blocking collectives  176 us (28%)
  starting transfers between devices  173 us (27%)
  other arithmetic  40.7 us (6%)
  local copies, waits for them, and re-layouts  17.2 us (3%)
  between operations  15.2 us (2%)
  matrix products  9.87 us (2%)
    ppermute x32, starting transfers between devices, passed_along(): lax.ppermute(value, axis, [(source, source + steps) for source in range(f...  161 us
    psum x1, blocking collectives, body(): all_states, all_tails = lax.psum((candidate, tail_rows), 'ctx')  130 us
    ppermute x32, waiting for transfers between devices, passed_along(): lax.ppermute(value, axis, [(source, source + steps) for source in range(f...  124 us
    psum x1, waiting for transfers between devices, body(): all_states, all_tails = lax.psum((candidate, tail_rows), 'ctx')  77.4 us
    psum x1, blocking collectives, finish(): total_squares = lax.psum(partial_squares, 'tp')  28.6 us
    add x31, other arithmetic, carry_step(): return passed_along(end_decay[:, None, None] * state + end_state, 'ctx', 1)  21.3 us
    all_gather x1, blocking collectives, body(): lax.all_gather(branch_bc, 'tp', axis=0, tiled=True)  17.5 us
  transfers between devices with their start and end apart: 34, of which 32 were waited for; matrix products, arithmetic and copies ran while one was open for 5% of the time, Pallas kernels for 0%

profile of v1, /device:TPU:1, one launch (start us, length us, event | category | flops | bytes accessed | tf_op | source)
XLA Modules:
  0.0 634.7 jit_solution(2501920792919413146)
XLA Ops:
  8.6 11.8 %all-to-all-start = ((bf16[16,16,256]{2,1,0:T(8,128)(2,1)}), bf16[16,16,256]{2,1,0:T(8,128)(2,1)S(1)}, u32[]{:S(2)}, u32[]{:S(2)}) async-start(bf16[16,16,256]{2,1,0:T(8,128)(2,1)} %stack.2), calls=%async_computation | async-start | bytes 262144 | tf_op jit(solution)/shard_map/all_to_all | solution.py:199
  35.8 17.5 %all_gather.3 = bf16[256,256]{1,0:T(8,128)(2,1)S(1)} all-gather(bf16[16,256]{1,0:T(8,128)(2,1)S(1)} %copy-done.29), channel_id=1, replica_groups=mesh['ctx'=32,'tp'=16] {'tp'}, dimensions={0}, use_global_device_ids=true | all-gather | bytes 139264 | tf_op jit(solution)/shard_map/all_gather | solution.py:210
  68.1 304.2 %while.10 = (s32[]{:T(128)}, f32[8,64,128]{2,1,0:T(8,128)S(1)}, f32[8]{0:T(128)}, f32[8,64,128]{2,1,0:T(8,128)S(1)}, s32[]{:T(128)}) while((s32[]{:T(128)}, f32[8,64,128]{2,1,0:T(8,128)S(1)}, f32[8]{0:T(128)}, f32[8,64,128]{2,1,0:T(8,128)S(1)}, s32[]{:T(128)}) %tuple.49), condition=%wide.region_3.4_spmd, body=%wide.region_2.3_spmd.sunk | while | flops 131074 | bytes 1835141 | solution.py:237
  137.6 5.3 collective-permute-start
  148.3 5.6 collective-permute-start
  153.9 5.7 collective-permute-done
  160.3 6.0 collective-permute-start
  166.3 5.3 collective-permute-done
  189.7 5.3 collective-permute-start
  199.0 5.3 collective-permute-start
  208.3 5.3 collective-permute-start
  236.5 5.5 collective-permute-start
  252.8 5.7 collective-permute-done
  263.3 5.6 collective-permute-done
  280.0 5.6 collective-permute-start
  291.3 7.3 %collective-permute-start = (f32[8,64,128]{2,1,0:T(8,128)S(1)}, f32[8,64,128]{2,1,0:T(8,128)S(1)}, u32[]{:S(2)}, u32[]{:S(2)}) collective-permute-start(f32[8,64,128]{2,1,0:T(8,128)S(1)} %multiply_add_fusion.4), channel_id=1, source_target_pairs={{0,16},{16,32},{32,48},{48,64},{64,80},{80,96},{96,112},{112,128},... | collective-permute-start | bytes 786440 | tf_op jit(solution)/shard_map/while/body/eval_jaxpr/ppermute | solution.py:14
  303.6 6.0 collective-permute-start
  313.6 5.8 collective-permute-start
  341.7 6.2 collective-permute-start
  351.9 6.2 collective-permute-start
  362.1 6.2 collective-permute-start
  377.9 130.2 %psum.29 = bf16[8,3,768]{2,1,0:T(4,128)(2,1)S(1)} all-reduce(f32[8,3,768]{2,1,0:T(4,128)S(1)} %reshape.514), channel_id=1, replica_groups=mesh['ctx'=32,'tp'=16] {'ctx'}, use_global_device_ids=true, to_apply=%region_14.15 | all-reduce | flops 18432 | bytes 110592 | tf_op jit(solution)/shard_map/psum | solution.py:258
  513.8 77.4 %all-reduce.6.cloned.1.call-done = f32[8,8,64,128]{3,2,1,0:T(8,128)} async-done(((f32[8,8,64,128]{3,2,1,0:T(8,128)}), f32[8,8,64,128]{3,2,1,0:T(8,128)}) %all-reduce.6.cloned.1.call-update) | async-done | bytes 2097168 | tf_op jit(solution)/shard_map/psum | solution.py:258
  597.4 28.6 %all-reduce.3 = (f32[256,1]{0,1:T(1,128)S(1)}, f32[256,1]{0,1:T(1,128)S(1)}) all-reduce(f32[256,1]{0,1:T(1,128)S(1)} %bitcast.104, f32[256,1]{0,1:T(1,128)S(1)} %bitcast.107), channel_id=1, replica_groups=mesh['ctx'=32,'tp'=16] {'tp'}, use_global_device_ids=true, to_apply=%region_5.6 | all-reduce | flops 512 | bytes 4096 | tf_op jit(solution)/shard_map/psum | solution.py:78
  (314 shorter events, 249.3 us)
Async XLA Ops:
  8.6 48.7 %all-to-all-start = ((bf16[16,16,256]{2,1,0:T(8,128)(2,1)}), bf16[16,16,256]{2,1,0:T(8,128)(2,1)S(1)}, u32[]{:S(2)}, u32[]{:S(2)}) async-start(bf16[16,16,256]{2,1,0:T(8,128)(2,1)} %stack.2), calls=%async_computation | async-start | bytes 262144 | tf_op jit(solution)/shard_map/all_to_all | solution.py:199
  20.5 570.7 %all-reduce.6.cloned.1.call-start = ((), (), s32[]{:S(2)}) async-start(), calls=%async_computation.1 | async-start | bytes 4194304 | tf_op jit(solution)/shard_map/psum | solution.py:258
  68.9 8.4 %collective-permute-start = (f32[8,64,128]{2,1,0:T(8,128)S(1)}, f32[8,64,128]{2,1,0:T(8,128)S(1)}, u32[]{:S(2)}, u32[]{:S(2)}) collective-permute-start(f32[8,64,128]{2,1,0:T(8,128)S(1)} %multiply_add_fusion.4), channel_id=1, source_target_pairs={{0,16},{16,32},{32,48},{48,64},{64,80},{80,96},{96,112},{112,128},... | collective-permute-start | bytes 786440 | tf_op jit(solution)/shard_map/while/body/eval_jaxpr/ppermute | solution.py:14
  128.2 8.6 %collective-permute-start = (f32[8,64,128]{2,1,0:T(8,128)S(1)}, f32[8,64,128]{2,1,0:T(8,128)S(1)}, u32[]{:S(2)}, u32[]{:S(2)}) collective-permute-start(f32[8,64,128]{2,1,0:T(8,128)S(1)} %multiply_add_fusion.4), channel_id=1, source_target_pairs={{0,16},{16,32},{32,48},{48,64},{64,80},{80,96},{96,112},{112,128},... | collective-permute-start | bytes 786440 | tf_op jit(solution)/shard_map/while/body/eval_jaxpr/ppermute | solution.py:14
  137.6 10.0 %collective-permute-start = (f32[8,64,128]{2,1,0:T(8,128)S(1)}, f32[8,64,128]{2,1,0:T(8,128)S(1)}, u32[]{:S(2)}, u32[]{:S(2)}) collective-permute-start(f32[8,64,128]{2,1,0:T(8,128)S(1)} %multiply_add_fusion.4), channel_id=1, source_target_pairs={{0,16},{16,32},{32,48},{48,64},{64,80},{80,96},{96,112},{112,128},... | collective-permute-start | bytes 786440 | tf_op jit(solution)/shard_map/while/body/eval_jaxpr/ppermute | solution.py:14
  148.3 11.3 %collective-permute-start = (f32[8,64,128]{2,1,0:T(8,128)S(1)}, f32[8,64,128]{2,1,0:T(8,128)S(1)}, u32[]{:S(2)}, u32[]{:S(2)}) collective-permute-start(f32[8,64,128]{2,1,0:T(8,128)S(1)} %multiply_add_fusion.4), channel_id=1, source_target_pairs={{0,16},{16,32},{32,48},{48,64},{64,80},{80,96},{96,112},{112,128},... | collective-permute-start | bytes 786440 | tf_op jit(solution)/shard_map/while/body/eval_jaxpr/ppermute | solution.py:14
  160.3 11.2 %collective-permute-start = (f32[8,64,128]{2,1,0:T(8,128)S(1)}, f32[8,64,128]{2,1,0:T(8,128)S(1)}, u32[]{:S(2)}, u32[]{:S(2)}) collective-permute-start(f32[8,64,128]{2,1,0:T(8,128)S(1)} %multiply_add_fusion.4), channel_id=1, source_target_pairs={{0,16},{16,32},{32,48},{48,64},{64,80},{80,96},{96,112},{112,128},... | collective-permute-start | bytes 786440 | tf_op jit(solution)/shard_map/while/body/eval_jaxpr/ppermute | solution.py:14
  172.2 8.6 %collective-permute-start = (f32[8,64,128]{2,1,0:T(8,128)S(1)}, f32[8,64,128]{2,1,0:T(8,128)S(1)}, u32[]{:S(2)}, u32[]{:S(2)}) collective-permute-start(f32[8,64,128]{2,1,0:T(8,128)S(1)} %multiply_add_fusion.4), channel_id=1, source_target_pairs={{0,16},{16,32},{32,48},{48,64},{64,80},{80,96},{96,112},{112,128},... | collective-permute-start | bytes 786440 | tf_op jit(solution)/shard_map/while/body/eval_jaxpr/ppermute | solution.py:14
  189.7 8.6 %collective-permute-start = (f32[8,64,128]{2,1,0:T(8,128)S(1)}, f32[8,64,128]{2,1,0:T(8,128)S(1)}, u32[]{:S(2)}, u32[]{:S(2)}) collective-permute-start(f32[8,64,128]{2,1,0:T(8,128)S(1)} %multiply_add_fusion.4), channel_id=1, source_target_pairs={{0,16},{16,32},{32,48},{48,64},{64,80},{80,96},{96,112},{112,128},... | collective-permute-start | bytes 786440 | tf_op jit(solution)/shard_map/while/body/eval_jaxpr/ppermute | solution.py:14
  199.0 8.6 %collective-permute-start = (f32[8,64,128]{2,1,0:T(8,128)S(1)}, f32[8,64,128]{2,1,0:T(8,128)S(1)}, u32[]{:S(2)}, u32[]{:S(2)}) collective-permute-start(f32[8,64,128]{2,1,0:T(8,128)S(1)} %multiply_add_fusion.4), channel_id=1, source_target_pairs={{0,16},{16,32},{32,48},{48,64},{64,80},{80,96},{96,112},{112,128},... | collective-permute-start | bytes 786440 | tf_op jit(solution)/shard_map/while/body/eval_jaxpr/ppermute | solution.py:14
  208.3 8.6 %collective-permute-start = (f32[8,64,128]{2,1,0:T(8,128)S(1)}, f32[8,64,128]{2,1,0:T(8,128)S(1)}, u32[]{:S(2)}, u32[]{:S(2)}) collective-permute-start(f32[8,64,128]{2,1,0:T(8,128)S(1)} %multiply_add_fusion.4), channel_id=1, source_target_pairs={{0,16},{16,32},{32,48},{48,64},{64,80},{80,96},{96,112},{112,128},... | collective-permute-start | bytes 786440 | tf_op jit(solution)/shard_map/while/body/eval_jaxpr/ppermute | solution.py:14
  226.7 9.1 %collective-permute-start = (f32[8,64,128]{2,1,0:T(8,128)S(1)}, f32[8,64,128]{2,1,0:T(8,128)S(1)}, u32[]{:S(2)}, u32[]{:S(2)}) collective-permute-start(f32[8,64,128]{2,1,0:T(8,128)S(1)} %multiply_add_fusion.4), channel_id=1, source_target_pairs={{0,16},{16,32},{32,48},{48,64},{64,80},{80,96},{96,112},{112,128},... | collective-permute-start | bytes 786440 | tf_op jit(solution)/shard_map/while/body/eval_jaxpr/ppermute | solution.py:14
  236.5 10.5 %collective-permute-start = (f32[8,64,128]{2,1,0:T(8,128)S(1)}, f32[8,64,128]{2,1,0:T(8,128)S(1)}, u32[]{:S(2)}, u32[]{:S(2)}) collective-permute-start(f32[8,64,128]{2,1,0:T(8,128)S(1)} %multiply_add_fusion.4), channel_id=1, source_target_pairs={{0,16},{16,32},{32,48},{48,64},{64,80},{80,96},{96,112},{112,128},... | collective-permute-start | bytes 786440 | tf_op jit(solution)/shard_map/while/body/eval_jaxpr/ppermute | solution.py:14
  247.7 10.8 %collective-permute-start = (f32[8,64,128]{2,1,0:T(8,128)S(1)}, f32[8,64,128]{2,1,0:T(8,128)S(1)}, u32[]{:S(2)}, u32[]{:S(2)}) collective-permute-start(f32[8,64,128]{2,1,0:T(8,128)S(1)} %multiply_add_fusion.4), channel_id=1, source_target_pairs={{0,16},{16,32},{32,48},{48,64},{64,80},{80,96},{96,112},{112,128},... | collective-permute-start | bytes 786440 | tf_op jit(solution)/shard_map/while/body/eval_jaxpr/ppermute | solution.py:14
  259.2 9.8 %collective-permute-start = (f32[8,64,128]{2,1,0:T(8,128)S(1)}, f32[8,64,128]{2,1,0:T(8,128)S(1)}, u32[]{:S(2)}, u32[]{:S(2)}) collective-permute-start(f32[8,64,128]{2,1,0:T(8,128)S(1)} %multiply_add_fusion.4), channel_id=1, source_target_pairs={{0,16},{16,32},{32,48},{48,64},{64,80},{80,96},{96,112},{112,128},... | collective-permute-start | bytes 786440 | tf_op jit(solution)/shard_map/while/body/eval_jaxpr/ppermute | solution.py:14
  269.7 9.6 %collective-permute-start = (f32[8,64,128]{2,1,0:T(8,128)S(1)}, f32[8,64,128]{2,1,0:T(8,128)S(1)}, u32[]{:S(2)}, u32[]{:S(2)}) collective-permute-start(f32[8,64,128]{2,1,0:T(8,128)S(1)} %multiply_add_fusion.4), channel_id=1, source_target_pairs={{0,16},{16,32},{32,48},{48,64},{64,80},{80,96},{96,112},{112,128},... | collective-permute-start | bytes 786440 | tf_op jit(solution)/shard_map/while/body/eval_jaxpr/ppermute | solution.py:14
  280.0 10.6 %collective-permute-start = (f32[8,64,128]{2,1,0:T(8,128)S(1)}, f32[8,64,128]{2,1,0:T(8,128)S(1)}, u32[]{:S(2)}, u32[]{:S(2)}) collective-permute-start(f32[8,64,128]{2,1,0:T(8,128)S(1)} %multiply_add_fusion.4), channel_id=1, source_target_pairs={{0,16},{16,32},{32,48},{48,64},{64,80},{80,96},{96,112},{112,128},... | collective-permute-start | bytes 786440 | tf_op jit(solution)/shard_map/while/body/eval_jaxpr/ppermute | solution.py:14
  291.3 11.6 %collective-permute-start = (f32[8,64,128]{2,1,0:T(8,128)S(1)}, f32[8,64,128]{2,1,0:T(8,128)S(1)}, u32[]{:S(2)}, u32[]{:S(2)}) collective-permute-start(f32[8,64,128]{2,1,0:T(8,128)S(1)} %multiply_add_fusion.4), channel_id=1, source_target_pairs={{0,16},{16,32},{32,48},{48,64},{64,80},{80,96},{96,112},{112,128},... | collective-permute-start | bytes 786440 | tf_op jit(solution)/shard_map/while/body/eval_jaxpr/ppermute | solution.py:14
  303.6 9.3 %collective-permute-start = (f32[8,64,128]{2,1,0:T(8,128)S(1)}, f32[8,64,128]{2,1,0:T(8,128)S(1)}, u32[]{:S(2)}, u32[]{:S(2)}) collective-permute-start(f32[8,64,128]{2,1,0:T(8,128)S(1)} %multiply_add_fusion.4), channel_id=1, source_target_pairs={{0,16},{16,32},{32,48},{48,64},{64,80},{80,96},{96,112},{112,128},... | collective-permute-start | bytes 786440 | tf_op jit(solution)/shard_map/while/body/eval_jaxpr/ppermute | solution.py:14
  313.6 9.1 %collective-permute-start = (f32[8,64,128]{2,1,0:T(8,128)S(1)}, f32[8,64,128]{2,1,0:T(8,128)S(1)}, u32[]{:S(2)}, u32[]{:S(2)}) collective-permute-start(f32[8,64,128]{2,1,0:T(8,128)S(1)} %multiply_add_fusion.4), channel_id=1, source_target_pairs={{0,16},{16,32},{32,48},{48,64},{64,80},{80,96},{96,112},{112,128},... | collective-permute-start | bytes 786440 | tf_op jit(solution)/shard_map/while/body/eval_jaxpr/ppermute | solution.py:14
  332.5 8.5 %collective-permute-start = (f32[8,64,128]{2,1,0:T(8,128)S(1)}, f32[8,64,128]{2,1,0:T(8,128)S(1)}, u32[]{:S(2)}, u32[]{:S(2)}) collective-permute-start(f32[8,64,128]{2,1,0:T(8,128)S(1)} %multiply_add_fusion.4), channel_id=1, source_target_pairs={{0,16},{16,32},{32,48},{48,64},{64,80},{80,96},{96,112},{112,128},... | collective-permute-start | bytes 786440 | tf_op jit(solution)/shard_map/while/body/eval_jaxpr/ppermute | solution.py:14
  341.7 9.5 %collective-permute-start = (f32[8,64,128]{2,1,0:T(8,128)S(1)}, f32[8,64,128]{2,1,0:T(8,128)S(1)}, u32[]{:S(2)}, u32[]{:S(2)}) collective-permute-start(f32[8,64,128]{2,1,0:T(8,128)S(1)} %multiply_add_fusion.4), channel_id=1, source_target_pairs={{0,16},{16,32},{32,48},{48,64},{64,80},{80,96},{96,112},{112,128},... | collective-permute-start | bytes 786440 | tf_op jit(solution)/shard_map/while/body/eval_jaxpr/ppermute | solution.py:14
  351.9 9.5 %collective-permute-start = (f32[8,64,128]{2,1,0:T(8,128)S(1)}, f32[8,64,128]{2,1,0:T(8,128)S(1)}, u32[]{:S(2)}, u32[]{:S(2)}) collective-permute-start(f32[8,64,128]{2,1,0:T(8,128)S(1)} %multiply_add_fusion.4), channel_id=1, source_target_pairs={{0,16},{16,32},{32,48},{48,64},{64,80},{80,96},{96,112},{112,128},... | collective-permute-start | bytes 786440 | tf_op jit(solution)/shard_map/while/body/eval_jaxpr/ppermute | solution.py:14
  362.1 10.2 %collective-permute-start = (f32[8,64,128]{2,1,0:T(8,128)S(1)}, f32[8,64,128]{2,1,0:T(8,128)S(1)}, u32[]{:S(2)}, u32[]{:S(2)}) collective-permute-start(f32[8,64,128]{2,1,0:T(8,128)S(1)} %multiply_add_fusion.4), channel_id=1, source_target_pairs={{0,16},{16,32},{32,48},{48,64},{64,80},{80,96},{96,112},{112,128},... | collective-permute-start | bytes 786440 | tf_op jit(solution)/shard_map/while/body/eval_jaxpr/ppermute | solution.py:14
  (69 other events, 3385.7 us)
Sparse Core Ops, SparseCore 0:
  374.9 216.2 all-reduce.5
